TPU v7x, 32 devices: a whole 2x2x4 slice. The times are simulated.
32 devices in a mesh: grp: 2 (over y), panel: 4 (over z), tok: 2 (over x), rep: 2 (over core).
Axes of the slice: x: 2, y: 2, z: 4, core: 2. Of those that a mesh axis runs over, the one named last changes fastest.
Arguments:
- grads: bfloat16 [8, 512, 32768], P(('grp', 'rep'), 'tok', 'panel'), parts along dimension 0, may hold values from -6 to 6
- acts: bfloat16 [8, 512, 8192], P(('grp', 'rep'), 'tok', 'panel'), parts along dimension 0, may hold values from -6 to 6
- out_basis: bfloat16 [32768, 256], P('panel', ('tok', 'rep')), may hold values from -0.03125 to 0.03125
- in_basis: bfloat16 [8192, 128], P('panel'), may hold values from -0.0625 to 0.0625
- eigvals: float32 [256, 128], P('panel'), may hold values from 0.05 to 5
- query_rot: bfloat16 [128, 256, 128], P('grp', 'panel'), parts along dimension 0, may hold values from -0.0014648438 to 0.0014648438
- lengths: int32 [8], P(('grp', 'rep')), parts along dimension 0, may hold values from 128 to 512
- token_mask: int32 [8, 512], P(('grp', 'rep'), 'tok'), parts along dimension 0, may hold values 0 or 1
- failure_ids: int32 [128], P('grp'), parts along dimension 0, may hold values from 0 to 7, as said below
Outputs:
- query_scores: float32 [64, 8], P(None, ('grp', 'rep')), parts along dimension 1
- influence: float32 [8, 8], P(None, ('grp', 'rep')), parts along dimension 1
There are 2 independent parts, one for each index of `grp`. A program takes and returns all parts, laid end to end along the dimension named above; an argument that names none is the same for every part. Nothing has to cross between parts.
Inputs may be any that keep to these rules, and one draw needn't show every extreme that they name: `failure_ids`: at least one failure other than 0 and 7 has no query.
All inputs are finite; a program needn't handle non-finite values. No bound on the sum of `token_mask` on one device may be relied on, other than what follows from the above.
Results may differ from a plain program's by a relative error of at most 0.0049.
Values may be sent and summed in bfloat16 or wider, within the bound.
A program may use at most 64 MiB of HBM per device.

v0:
```python
import jax
import jax.numpy as jnp
from jax import lax
from jax.sharding import PartitionSpec as P

NFAIL = 8


damping = 0.1


def per_device(
    grads, acts, out_basis, in_basis, eigvals, query_rot, lengths, token_mask, failure_ids
):
    seq_dev, len_dev, ff_dev = grads.shape
    rows = seq_dev * len_dev
    grad_rows = grads.reshape(rows, ff_dev)
    act_rows = acts.reshape(rows, acts.shape[2])
    ks_dev = eigvals.shape[0]
    proj_part = jnp.dot(
        grad_rows,
        lax.all_gather(out_basis, ("tok", "rep"), axis=1, tiled=True),
        preferred_element_type=jnp.float32,
    )
    in_part = jnp.dot(act_rows, in_basis, preferred_element_type=jnp.float32)
    proj_all, proj_in = lax.psum((proj_part, in_part), "panel")
    proj_out = lax.dynamic_slice_in_dim(proj_all, lax.axis_index("panel") * ks_dev, ks_dev, 1)
    proj_low = proj_in.astype(jnp.bfloat16)
    weighted = (query_rot.astype(jnp.float32) / (eigvals + damping)).astype(jnp.bfloat16)
    mixed = jnp.einsum("qkl,tl->qkt", weighted, proj_low, preferred_element_type=jnp.float32)
    token_score = jnp.einsum("qkt,tk->qt", mixed, proj_out, precision=lax.Precision.HIGHEST)
    positions = lax.axis_index("tok") * len_dev + jnp.arange(len_dev, dtype=jnp.int32)
    valid = ((positions[None, :] < lengths[:, None]) & (token_mask == 1)).astype(jnp.float32)
    queries = weighted.shape[0]
    partial_scores = jnp.sum(
        token_score.reshape(queries, seq_dev, len_dev) * valid[None, :, :], axis=2
    )
    query_scores = lax.psum(partial_scores, ("panel", "tok"))
    onehot = (failure_ids[None, :] == jnp.arange(NFAIL, dtype=jnp.int32)[:, None]).astype(
        jnp.float32
    )
    counts = jnp.maximum(jnp.sum(onehot, axis=1), 1.0)
    influence = jnp.dot(onehot, query_scores, precision=lax.Precision.HIGHEST) / counts[:, None]
    return (query_scores, influence)


def solution(mesh):
    in_specs = (
        P(("grp", "rep"), "tok", "panel"),
        P(("grp", "rep"), "tok", "panel"),
        P("panel", ("tok", "rep")),
        P("panel", None),
        P("panel", None),
        P("grp", "panel", None),
        P(("grp", "rep")),
        P(("grp", "rep"), "tok"),
        P("grp"),
    )
    out_specs = (P(None, ("grp", "rep")), P(None, ("grp", "rep")))
    return jax.shard_map(
        per_device, mesh=mesh, in_specs=in_specs, out_specs=out_specs, check_vma=False
    )
```

profile of v0, /device:TPU:0, one launch (start us, length us, event | category | flops | bytes accessed | tf_op | source)
XLA Modules:
  0.0 128.5 jit_solution(18417730445821571451)
XLA Ops:
  7.2 0.0 copy-start
  7.2 0.0 all-gather.2.cloned.1.call-start
  7.2 0.7 all-gather.2.cloned.1.call-update
  7.9 0.0 all-reduce.3.cloned.1.call-start
  8.0 0.8 convert_reduce_fusion
  8.7 0.8 and_convert_fusion
  9.5 0.0 copy-done
  9.5 1.7 %fusion.4 = f32[512,128]{1,0:T(8,128)S(1)} fusion(bf16[512,2048]{1,0:T(8,128)(2,1)S(1)} %bitcast.13, bf16[2048,128]{1,0:T(8,128)(2,1)} %param.12), kind=kOutput, calls=%fused_computation.15 | convolution fusion | flops 268435456 | bytes 2883584 | tf_op jit(solution)/shard_map/dot_general | solution.py:25
  11.3 35.5 %all-gather.2.cloned.1.call-done = bf16[8192,256]{0,1:T(8,128)(2,1)} async-done(((bf16[8192,64]{0,1:T(8,128)(2,1)}), bf16[8192,256]{0,1:T(8,128)(2,1)}) %all-gather.2.cloned.1.call-update) | async-done | bytes 4194320 | tf_op jit(solution)/shard_map/all_gather | solution.py:22
  46.8 0.0 copy-start.1
  46.8 7.7 %fusion.3 = f32[512,256]{0,1:T(8,128)} fusion(bf16[512,8192]{1,0:T(8,128)(2,1)} %bitcast.15, bf16[8192,256]{0,1:T(8,128)(2,1)} %all-gather.2.cloned.1.call-done), kind=kOutput, calls=%fused_computation.14 | convolution fusion | flops 2147483648 | bytes 13107200 | tf_op jit(solution)/shard_map/dot_general | solution.py:20
  54.5 0.0 all-reduce.3.cloned.1.call-update
  54.6 0.0 copy-done.1
  54.6 28.4 %all-reduce.4 = bf16[512,128]{1,0:T(8,128)(2,1)S(1)} all-reduce(f32[512,128]{1,0:T(8,128)S(1)} %fusion.4), channel_id=1, replica_groups=mesh['grp'=2,'panel'=4,'tok'=2,'rep'=2] {'panel'}, use_global_device_ids=true, to_apply=%region_1.0 | all-reduce | flops 65536 | bytes 393216 | tf_op jit(solution)/shard_map/psum | solution.py:26
  83.0 13.7 %all-reduce.3.cloned.1.call-done = f32[512,256]{0,1:T(8,128)} async-done(((f32[512,256]{0,1:T(8,128)}), f32[512,256]{0,1:T(8,128)}) %all-reduce.3.cloned.1.call-update) | async-done | bytes 524304 | tf_op jit(solution)/shard_map/psum | solution.py:26
  96.7 0.9 constant_dynamic-slice_fusion
  97.6 0.0 copy-start.3
  97.6 2.5 %multiply_reduce_fusion = f32[512,64]{0,1:T(8,128)S(1)} fusion(f32[512,64]{0,1:T(8,128)S(1)} %constant_dynamic-slice_fusion, bf16[64,64,128]{2,1,0:T(8,128)(2,1)} %param.14, f32[64,128]{1,0:T(8,128)S(1)} %broadcast_add_fusion, bf16[512,128]{1,0:T(8,128)(2,1)S(1)} %all-reduce.4), kind=kOutput, calls=%fused_computation | convolution fusion | flops 542605312 | bytes 1474560 | tf_op jit(solution)/shard_map/qkl,tl->qkt/dot_general | solution.py:30
  100.2 0.1 reshape.26
  100.3 0.1 multiply_reduce_fusion.1
  100.4 0.1 copy.17
  100.5 20.5 %psum.23 = f32[64,2]{0,1:T(2,128)S(1)} all-reduce(f32[64,2]{0,1:T(2,128)S(1)} %copy.17), channel_id=1, replica_groups=mesh['grp'=2,'panel'=4,'tok'=2,'rep'=2] {'panel','tok'}, use_global_device_ids=true, to_apply=%region_3.0 | all-reduce | flops 128 | bytes 1024 | tf_op jit(solution)/shard_map/psum | solution.py:38
  120.9 0.0 copy-done.3
  120.9 0.0 copy-start.2
  120.9 0.7 convolution_divide_fusion
  121.6 0.0 copy-done.2
  (3 shorter events, 0.0 us)
Async XLA Ops:
  7.2 2.3 %copy-start = (bf16[2,256,2048]{2,1,0:T(8,128)(2,1)S(1)}, bf16[2,256,2048]{2,1,0:T(8,128)(2,1)}, u32[]{:S(2)}) copy-start(bf16[2,256,2048]{2,1,0:T(8,128)(2,1)} %param.10) | copy-start | bytes 6291460
  7.2 39.6 %all-gather.2.cloned.1.call-start = ((), (), s32[]{:S(2)}) async-start(), calls=%async_computation | async-start | bytes 5242880 | tf_op jit(solution)/shard_map/all_gather | solution.py:22
  7.9 88.8 %all-reduce.3.cloned.1.call-start = ((), (), s32[]{:S(2)}) async-start(), calls=%async_computation.1 | async-start | bytes 1048576 | tf_op jit(solution)/shard_map/psum | solution.py:26
  46.8 7.8 %copy-start.1 = (f32[64,128]{1,0:T(8,128)S(1)}, f32[64,128]{1,0:T(8,128)}, u32[]{:S(2)}) copy-start(f32[64,128]{1,0:T(8,128)} %param.13) | copy-start | bytes 98308
  97.6 23.3 %copy-start.3 = (s32[64]{0:T(128)S(1)}, s32[64]{0:T(128)}, u32[]{:S(2)}) copy-start(s32[64]{0:T(128)} %param.17) | copy-start | bytes 772
  120.9 0.7 copy-start.2
Sparse Core Ops, SparseCore 0:
  9.6 37.1 all-gather.1
  54.7 41.9 all-reduce.2
where the time goes:
time: 129 us; the launch traced here: 128 us
  waiting for transfers between devices  50 us (39%)
  blocking collectives  48.8 us (38%)
  between operations  14.1 us (11%)
  matrix products  12.7 us (10%)
  other arithmetic  1.68 us (1%)
    all_gather x1, waiting for transfers between devices, per_device(): lax.all_gather(out_basis, ('tok', 'rep'), axis=1, tiled=True)  35.5 us
    psum x1, blocking collectives, per_device(): proj_all, proj_in = lax.psum((proj_part, in_part), 'panel')  28.4 us
    psum x1, blocking collectives, per_device(): query_scores = lax.psum(partial_scores, ('panel', 'tok'))  20.5 us
    psum x1, waiting for transfers between devices, per_device(): proj_all, proj_in = lax.psum((proj_part, in_part), 'panel')  13.7 us
    dot_general x1, matrix products, per_device(): jnp.dot(grad_rows, lax.all_gather(out_basis, ('tok', 'rep'), axis=1, tile...  7.74 us
  transfers between devices with their start and end apart: 2, of which 2 were waited for; matrix products, arithmetic and copies ran while one was open for 3% of the time, Pallas kernels for 0%

commit v1 on v0

v1 whole, which is shorter than its diff:
```python
import functools

import jax
import jax.numpy as jnp
from jax import lax
from jax.experimental import pallas as pl
from jax.experimental.pallas import tpu as pltpu
from jax.sharding import PartitionSpec as P

NFAIL = 8
DAMPING = 0.1
MESH = pl.DeviceIdType.MESH
F32 = jnp.float32
BF16 = jnp.bfloat16
NT = (((1,), (1,)), ((), ()))
TN = (((0,), (0,)), ((), ()))


def each(count, body):
    if count <= 8:
        for index in range(count):
            body(index)
    else:
        pl.loop(0, count)(body)


def kernel(
    sizes,
    grads_hbm, acts_hbm, basis_hbm, inb_hbm, eig_ref, qrot_hbm, len_ref, mask_ref, fail_ref,
    score_ref, infl_ref,
    grads, acts, inb, basis, qrot, weight, proj, in_send, in_recv, pin, pinv,
    m_send, m_recv, m_sum, s_send, s_recv,
    load_sem, grad_sem, own_send, own_recv, x_send, x_recv, y_send, y_recv,
    cx_send, cx_recv, cy_send, cy_recv,
    a_send, a_recv, g_send, g_recv, ms_sem, mr_sem, ss_sem, sr_sem,
):
    np_, nt, nc, ngrad = sizes
    grp, panel = lax.axis_index("grp"), lax.axis_index("panel")
    tok, rep = lax.axis_index("tok"), lax.axis_index("rep")
    seqs, length, hidden = grads.shape
    rows = seqs * length
    queries, kb, ka = qrot.shape
    cols = basis_hbm.shape[0]
    pair = 2 * cols
    npc = pair // kb
    half = hidden // 2
    cw = half // nc
    prow = rows // np_
    gstep = hidden // ngrad

    loads = [
        pltpu.make_async_copy(acts_hbm, acts, load_sem.at[0]),
        pltpu.make_async_copy(inb_hbm, inb, load_sem.at[1]),
        pltpu.make_async_copy(qrot_hbm, qrot, load_sem.at[2]),
    ]
    own_rows = pl.ds(pl.multiple_of((tok * 2 + rep) * cols, cols), cols)
    own_load = pltpu.make_async_copy(basis_hbm, basis.at[own_rows], load_sem.at[3])
    loads[0].start()
    loads[1].start()

    barrier = pltpu.get_barrier_semaphore()
    pl.semaphore_signal(barrier, inc=1, device_id={"rep": 1 - rep}, device_id_type=MESH)
    pl.semaphore_signal(barrier, inc=1, device_id={"grp": 1 - grp}, device_id_type=MESH)

    def other(index):
        shift = index + 1
        dp, dt = shift // nt, shift % nt
        return lax.rem(panel + dp, np_), lax.rem(tok + dt, nt)

    def greet(index):
        p, t = other(index)
        pl.semaphore_signal(barrier, inc=1, device_id={"panel": p, "tok": t}, device_id_type=MESH)

    each(np_ * nt - 1, greet)
    own_load.start()
    grad_loads = []
    for g in range(ngrad):
        at = pl.ds(g * gstep, gstep)
        grad_loads.append(
            pltpu.make_async_copy(grads_hbm.at[:, :, at], grads.at[:, :, at], grad_sem.at[g])
        )
    for copy in grad_loads:
        copy.start()
    loads[2].start()
    pl.semaphore_wait(barrier, np_ * nt + 1)

    def lanes(part, i):
        return pl.ds(pl.multiple_of(part * half + i * cw, cw), cw)

    def block(t, r):
        return pl.ds(pl.multiple_of((t * 2 + r) * cols, cols), cols)

    def remote(src, dst, send, recv, where):
        return pltpu.make_async_remote_copy(
            src_ref=src, dst_ref=dst, send_sem=send, recv_sem=recv,
            device_id=where, device_id_type=MESH,
        )

    def x_copy(d, i):
        at = lanes(grp, i)
        return remote(
            basis_hbm.at[:, at], basis.at[own_rows, at], x_send.at[d, i], x_recv.at[d, i],
            {"tok": lax.rem(tok + d + 1, nt)},
        )

    def from_tok(d):
        return lax.rem(tok + nt - d - 1, nt)

    def pass_copy(d, i, part, r, send, recv, where):
        at = basis.at[block(from_tok(d), r), lanes(part, i)]
        return remote(at, at, send.at[d, i], recv.at[d, i], where)

    def y_copy(d, i, part):
        return pass_copy(d, i, part, rep, y_send, y_recv, {"grp": 1 - grp})

    def cx_copy(d, i, r):
        return pass_copy(d, i, grp, r, cx_send, cx_recv, {"rep": 1 - rep})

    def cy_copy(d, i, r):
        return pass_copy(d, i, 1 - grp, r, cy_send, cy_recv, {"rep": 1 - rep})

    own_copy = remote(basis_hbm, basis.at[own_rows], own_send, own_recv, {"rep": 1 - rep})
    for i in range(nc):
        for d in range(nt - 1):
            x_copy(d, i).start()
        if i == 0:
            own_copy.start()

    loads[0].wait()
    loads[1].wait()
    in_part = jnp.dot(
        acts[...].reshape(rows, acts.shape[2]), inb[...], preferred_element_type=F32
    )
    in_send[...] = in_part.astype(BF16)

    def rows_of(p):
        return pl.ds(pl.multiple_of(p * prow, prow), prow)

    def a_copy(p):
        return remote(
            in_send.at[rows_of(p)], in_recv.at[panel], a_send.at[p], a_recv.at[panel],
            {"panel": p},
        )

    def a_from(p):
        return remote(
            in_send.at[rows_of(p)], in_recv.at[p], a_send.at[p], a_recv.at[p], {"panel": p}
        )

    def g_copy(p):
        mine = pin.at[rows_of(panel)]
        return remote(mine, mine, g_send.at[p], g_recv.at[panel], {"panel": p})

    def g_from(p):
        theirs = pin.at[rows_of(p)]
        return remote(theirs, theirs, g_send.at[p], g_recv.at[p], {"panel": p})

    def panels(body):
        each(np_ - 1, lambda index: body(lax.rem(panel + index + 1, np_)))

    panels(lambda p: a_copy(p).start())

    def sum_in():
        panels(lambda p: a_from(p).wait_recv())
        in_recv[panel] = in_send[rows_of(panel), :]
        total = in_recv[0].astype(F32)
        for p in range(1, np_):
            total = total + in_recv[p].astype(F32)
        pin[rows_of(panel), :] = total.astype(BF16)
        panels(lambda p: g_copy(p).start())

    def weigh():
        loads[2].wait()
        inverse = 1.0 / (eig_ref[...] + DAMPING)
        for q in range(0, queries, 8):
            w = qrot[q : q + 8].astype(F32) * inverse[None]
            w = w.astype(BF16).astype(F32)
            weight[:, q : q + 8, :] = jnp.swapaxes(w, 0, 1)
        s_send[...] = jnp.zeros_like(s_send)
        for copy in grad_loads:
            copy.wait()

    def valid_in():
        panels(lambda p: g_from(p).wait_recv())
        spots = lax.broadcasted_iota(jnp.int32, (1, length), 1) + tok * length
        for s in range(seqs):
            keep = jnp.where((spots < len_ref[s]) & (mask_ref[s : s + 1, :] == 1), 1.0, 0.0)
            keep = jnp.broadcast_to(keep, (ka, length)).T.astype(BF16)
            at = pl.ds(s * length, length)
            pinv[at, :] = pin[at, :] * keep

    def add_proj(d, part_rows, at, first):
        value = lax.dot_general(
            grads[:, :, at].reshape(rows, at.size), basis[part_rows, at], NT,
            preferred_element_type=F32,
        )
        if first:
            proj[d] = value
        else:
            proj[d] += value

    def pair_rows(t):
        return pl.ds(pl.multiple_of(t * pair, pair), pair)

    def m_copy(p):
        return remote(
            m_send.at[p], m_recv.at[panel], ms_sem.at[p], mr_sem.at[panel], {"panel": p}
        )

    def m_from(p):
        return remote(m_send.at[p], m_recv.at[p], ms_sem.at[p], mr_sem.at[p], {"panel": p})

    def mix(d, t):
        for s in range(seqs):
            at = pl.ds(s * length, length)
            m = lax.dot_general(
                proj[d, at, :].astype(BF16), pinv[at, :], TN, preferred_element_type=F32
            )
            m_send[pl.ds(t * npc, npc), s] = m.astype(BF16).reshape(npc, kb, ka)
        for j in range(npc):
            p = t * npc + j

            @pl.when(p != panel)
            def _():
                m_copy(p).start()

            @pl.when(p == panel)
            def _():
                m_recv[p] = m_send[p]

    def own_proj():
        own_load.wait()
        own_copy.wait_recv()
        for g in range(ngrad):
            add_proj(0, pair_rows(tok), pl.ds(g * gstep, gstep), g == 0)

    def own_mix():
        valid_in()
        mix(0, tok)

    tasks = {0: [weigh], min(1, nc - 1): [sum_in], min(2, nc - 1): [own_proj]}
    tasks.setdefault(min(4, nc - 1), []).append(own_mix)
    for i in range(nc):
        for d in range(nt - 1):
            x_arrive = remote(
                basis_hbm.at[:, lanes(grp, i)], basis.at[block(from_tok(d), rep), lanes(grp, i)],
                x_send.at[d, i], x_recv.at[d, i], {"tok": from_tok(d)},
            )
            x_arrive.wait_recv()
            y_copy(d, i, grp).start()
            cx_copy(d, i, rep).start()
        for task in tasks.get(i, ()):
            task()
        for d in range(nt - 1):
            y_copy(d, i, 1 - grp).wait_recv()
            cy_copy(d, i, rep).start()
        for d in range(nt - 1):
            t = from_tok(d)
            cx_copy(d, i, 1 - rep).wait_recv()
            add_proj(d + 1, pair_rows(t), lanes(grp, i), i == 0)
            cy_copy(d, i, 1 - rep).wait_recv()
            add_proj(d + 1, pair_rows(t), lanes(1 - grp, i), False)
    for d in range(nt - 1):
        mix(d + 1, from_tok(d))

    panels(lambda p: m_from(p).wait_recv())
    total = m_recv[0].astype(F32)
    for p in range(1, np_):
        total = total + m_recv[p].astype(F32)
    m_sum[...] = total

    def step(k8, sums):
        sums = list(sums)
        for j in range(8):
            k = k8 * 8 + j
            w = weight[k]
            for s in range(seqs):
                sums[s] = sums[s] + w * m_sum[s, pl.ds(k, 1), :]
        return tuple(sums)

    sums = lax.fori_loop(
        0, kb // 8, step, tuple(jnp.zeros((queries, ka), F32) for _ in range(seqs))
    )
    ones = jnp.ones((8, ka), F32)
    for s in range(seqs):
        line = lax.dot_general(
            ones, sums[s], NT, precision=lax.Precision.HIGHEST, preferred_element_type=F32
        )
        s_send[s : s + 1, 0:queries] = line[0:1, :]

    me = panel * nt + tok

    def s_copy(index):
        p, t = other(index)
        return remote(
            s_send, s_recv.at[me], ss_sem.at[index], sr_sem.at[me], {"panel": p, "tok": t}
        )

    def s_from(index):
        p, t = other(index)
        who = p * nt + t
        return remote(
            s_send, s_recv.at[who], ss_sem.at[index], sr_sem.at[who], {"panel": p, "tok": t}
        )

    each(np_ * nt - 1, lambda index: s_copy(index).start())
    s_recv[me] = s_send[...]
    each(np_ * nt - 1, lambda index: s_from(index).wait_recv())
    scores = s_recv[0]
    for who in range(1, np_ * nt):
        scores = scores + s_recv[who]
    scores = scores[:, 0:queries]
    score_ref[...] = scores[0:seqs, :]
    hot = jnp.where(
        lax.broadcasted_iota(jnp.int32, (NFAIL, queries), 0) == fail_ref[...], 1.0, 0.0
    )
    sums_f = lax.dot_general(
        scores, hot, NT, precision=lax.Precision.HIGHEST, preferred_element_type=F32
    )
    counts = lax.dot_general(
        jnp.ones((8, queries), F32), hot, NT, precision=lax.Precision.HIGHEST,
        preferred_element_type=F32,
    )
    infl_ref[...] = (sums_f / jnp.maximum(counts, 1.0))[0:seqs, :]

    own_copy.wait_send()
    for i in range(nc):
        for d in range(nt - 1):
            x_copy(d, i).wait_send()
            y_copy(d, i, grp).wait_send()
            cx_copy(d, i, rep).wait_send()
            cy_copy(d, i, rep).wait_send()
    panels(lambda p: a_copy(p).wait_send())
    panels(lambda p: g_copy(p).wait_send())
    panels(lambda p: m_copy(p).wait_send())
    each(np_ * nt - 1, lambda index: s_copy(index).wait_send())


def per_device(
    np_, nt, grads, acts, out_basis, in_basis, eigvals, query_rot, lengths, token_mask, failure_ids
):
    seqs, length, hidden = grads.shape
    rows = seqs * length
    queries, kb, ka = query_rot.shape
    cols = out_basis.shape[1]
    nc = min(8, hidden // 256)
    ngrad = min(8, hidden // 256)
    dma = pltpu.SemaphoreType.DMA
    hop = (nt - 1, nc)
    scratch = [
        pltpu.VMEM(grads.shape, BF16),
        pltpu.VMEM(acts.shape, BF16),
        pltpu.VMEM(in_basis.shape, BF16),
        pltpu.VMEM((cols * nt * 2, hidden), BF16),
        pltpu.VMEM(query_rot.shape, BF16),
        pltpu.VMEM((kb, queries, ka), F32),
        pltpu.VMEM((nt, rows, 2 * cols), F32),
        pltpu.VMEM((rows, ka), BF16),
        pltpu.VMEM((np_, rows // np_, ka), BF16),
        pltpu.VMEM((rows, ka), BF16),
        pltpu.VMEM((rows, ka), BF16),
        pltpu.VMEM((np_, seqs, kb, ka), BF16),
        pltpu.VMEM((np_, seqs, kb, ka), BF16),
        pltpu.VMEM((seqs, kb, ka), F32),
        pltpu.VMEM((8, 128), F32),
        pltpu.VMEM((np_ * nt, 8, 128), F32),
        dma((4,)),
        dma((ngrad,)),
        dma, dma,
        dma(hop), dma(hop), dma(hop), dma(hop),
        dma(hop), dma(hop), dma(hop), dma(hop),
        dma((np_,)), dma((np_,)), dma((np_,)), dma((np_,)),
        dma((np_,)), dma((np_,)),
        dma((np_ * nt,)), dma((np_ * nt,)),
    ]
    hbm = pl.BlockSpec(memory_space=pl.ANY)
    vmem = pl.BlockSpec(memory_space=pltpu.VMEM)
    scores, influence = pl.pallas_call(
        functools.partial(kernel, (np_, nt, nc, ngrad)),
        out_shape=(
            jax.ShapeDtypeStruct((seqs, queries), F32),
            jax.ShapeDtypeStruct((seqs, NFAIL), F32),
        ),
        in_specs=[
            hbm, hbm, hbm, hbm, vmem, hbm, pl.BlockSpec(memory_space=pltpu.SMEM), vmem, vmem
        ],
        out_specs=(vmem, vmem),
        scratch_shapes=scratch,
        compiler_params=pltpu.CompilerParams(
            collective_id=0, has_side_effects=True, vmem_limit_bytes=56 * 1024 * 1024
        ),
        name="influence",
    )(
        grads, acts, out_basis.T, in_basis, eigvals, query_rot, lengths, token_mask,
        failure_ids[None, :],
    )
    return scores.T, influence.T


def solution(mesh):
    in_specs = (
        P(("grp", "rep"), "tok", "panel"),
        P(("grp", "rep"), "tok", "panel"),
        P("panel", ("tok", "rep")),
        P("panel", None),
        P("panel", None),
        P("grp", "panel", None),
        P(("grp", "rep")),
        P(("grp", "rep"), "tok"),
        P("grp"),
    )
    out_specs = (P(None, ("grp", "rep")), P(None, ("grp", "rep")))
    return jax.shard_map(
        functools.partial(per_device, mesh.shape["panel"], mesh.shape["tok"]),
        mesh=mesh, in_specs=in_specs, out_specs=out_specs, check_vma=False,
    )
```

time: 129 us -> 64.8 us (0.50)
  Pallas kernels: 0 us -> 61.5 us
  waiting for transfers between devices: 50 us -> 0 us
  blocking collectives: 48.8 us -> 0 us
  between operations: 14.1 us -> 0.64 us
  matrix products: 12.7 us -> 0 us
  other arithmetic: 1.68 us -> 0 us
  local copies, waits for them, and re-layouts: 1.09 us -> 2.44 us
    pallas_call x0 -> x1, Pallas kernels: none -> 61.5 us  [per_device(): pl.pallas_call(functools.partial(kernel, (np_, nt, nc, ngrad)), out_shape...]
    psum x2 -> x0, blocking collectives: 48.8 us -> none  [the longest x1 28.4 us: per_device(): proj_all, proj_in = lax.psum((proj_part, in_part), 'panel')]
    all_gather x1 -> x0, waiting for transfers between devices: 35.5 us -> none  [per_device(): lax.all_gather(out_basis, ('tok', 'rep'), axis=1, tiled=True)]
    psum x1 -> x0, waiting for transfers between devices: 13.7 us -> none  [per_device(): proj_all, proj_in = lax.psum((proj_part, in_part), 'panel')]
    dot_general x4 -> x0, matrix products: 12.7 us -> none  [the longest x1 7.74 us: per_device(): jnp.dot(grad_rows, lax.all_gather(out_basis, ('tok', 'rep'), axis=1, tile...]
    unnamed x9 -> x2, local copies, waits for them, and re-layouts: 0.09 us -> 2.44 us
  transfers between devices with their start and end apart: 2 -> 0, of which waited for: 2 -> 0; matrix products, arithmetic and copies ran while one was open for 3% -> 0% of each run, Pallas kernels for 0% -> 0%
where the time goes in v1:
time: 64.8 us; the launch traced here: 64.6 us
  Pallas kernels  61.5 us (95%)
  local copies, waits for them, and re-layouts  2.44 us (4%)
    pallas_call x1, Pallas kernels, per_device(): pl.pallas_call(functools.partial(kernel, (np_, nt, nc, ngrad)), out_shape...  61.5 us
    unnamed x2, local copies, waits for them, and re-layouts  2.44 us

profile of v1, /device:TPU:0, one launch (start us, length us, event | category | flops | bytes accessed | tf_op | source)
XLA Modules:
  0.0 64.6 jit_solution(8699984582747046203)
XLA Ops:
  0.6 61.5 %influence.1 = (f32[2,64]{1,0:T(2,128)}, f32[2,8]{1,0:T(2,128)}) custom-call(bf16[2,256,8192]{2,1,0:T(8,128)(2,1)} %grads_hbm.1, bf16[2,256,2048]{2,1,0:T(8,128)(2,1)} %acts_hbm.1, bf16[64,8192]{1,0:T(8,128)(2,1)} %bitcast.4, bf16[2048,128]{1,0:T(8,128)(2,1)} %inb_hbm.1, f32[64,128]{1,0:T(8,128)} %eig_ref.1, bf16[64,64,128]{2,1,0:T(8,128)(2,1)} %qrot_hbm.1, ...), custom_call_target="tpu_custom_call" | custom-call | tf_op jit(solution)/shard_map/influence/pallas_call | solution.py:378
  62.1 1.2 %copy.13 = f32[64,2]{0,1:T(2,128)} copy(f32[64,2]{0,1:T(2,128)} %bitcast.6) | data formatting | bytes 1024
  63.4 1.2 %copy.14 = f32[8,2]{0,1:T(2,128)} copy(f32[8,2]{0,1:T(2,128)} %bitcast.5) | data formatting | bytes 128

commit v2 on v1

--- a/solution.py
+++ b/solution.py
@@ -26,11 +26,11 @@
 
 def kernel(
     sizes,
-    grads_hbm, acts_hbm, basis_hbm, inb_hbm, eig_ref, qrot_hbm, len_ref, mask_ref, fail_ref,
-    score_ref, infl_ref,
+    grads_hbm, acts_hbm, basis_hbm, inb_hbm, eig_ref, qrot_hbm, len_ref, mask_ref,
+    total_ref,
     grads, acts, inb, basis, qrot, weight, proj, in_send, in_recv, pin, pinv,
     m_send, m_recv, m_sum, s_send, s_recv,
-    load_sem, grad_sem, own_send, own_recv, x_send, x_recv, y_send, y_recv,
+    load_sem, grad_sem, own_sem, own_send, own_recv, x_send, x_recv, y_send, y_recv,
     cx_send, cx_recv, cy_send, cy_recv,
     a_send, a_recv, g_send, g_recv, ms_sem, mr_sem, ss_sem, sr_sem,
 ):
@@ -54,7 +54,15 @@
         pltpu.make_async_copy(qrot_hbm, qrot, load_sem.at[2]),
     ]
     own_rows = pl.ds(pl.multiple_of((tok * 2 + rep) * cols, cols), cols)
-    own_load = pltpu.make_async_copy(basis_hbm, basis.at[own_rows], load_sem.at[3])
+    own_loads = []
+    for j in range(2 * nc):
+        own_loads.append(
+            pltpu.make_async_copy(
+                basis_hbm.at[:, pl.ds(j * cw, cw)], basis.at[j, own_rows], own_sem.at[j]
+            )
+        )
+    for copy in own_loads:
+        copy.start()
     loads[0].start()
     loads[1].start()
 
@@ -72,7 +80,6 @@
         pl.semaphore_signal(barrier, inc=1, device_id={"panel": p, "tok": t}, device_id_type=MESH)
 
     each(np_ * nt - 1, greet)
-    own_load.start()
     grad_loads = []
     for g in range(ngrad):
         at = pl.ds(g * gstep, gstep)
@@ -84,9 +91,6 @@
     loads[2].start()
     pl.semaphore_wait(barrier, np_ * nt + 1)
 
-    def lanes(part, i):
-        return pl.ds(pl.multiple_of(part * half + i * cw, cw), cw)
-
     def block(t, r):
         return pl.ds(pl.multiple_of((t * 2 + r) * cols, cols), cols)
 
@@ -97,9 +101,9 @@
         )
 
     def x_copy(d, i):
-        at = lanes(grp, i)
-        return remote(
-            basis_hbm.at[:, at], basis.at[own_rows, at], x_send.at[d, i], x_recv.at[d, i],
+        mine = basis.at[grp * nc + i, own_rows]
+        return remote(
+            mine, mine, x_send.at[d, i], x_recv.at[d, i],
             {"tok": lax.rem(tok + d + 1, nt)},
         )
 
@@ -107,7 +111,7 @@
         return lax.rem(tok + nt - d - 1, nt)
 
     def pass_copy(d, i, part, r, send, recv, where):
-        at = basis.at[block(from_tok(d), r), lanes(part, i)]
+        at = basis.at[part * nc + i, block(from_tok(d), r)]
         return remote(at, at, send.at[d, i], recv.at[d, i], where)
 
     def y_copy(d, i, part):
@@ -119,19 +123,23 @@
     def cy_copy(d, i, r):
         return pass_copy(d, i, 1 - grp, r, cy_send, cy_recv, {"rep": 1 - rep})
 
-    own_copy = remote(basis_hbm, basis.at[own_rows], own_send, own_recv, {"rep": 1 - rep})
-    for i in range(nc):
+    own_copy = remote(basis.at[:, own_rows], basis.at[:, own_rows], own_send, own_recv, {"rep": 1 - rep})
+    for copy in own_loads:
+        copy.wait()
+
+    @pl.loop(0, nc)
+    def _(i):
         for d in range(nt - 1):
             x_copy(d, i).start()
-        if i == 0:
-            own_copy.start()
+
+    own_copy.start()
 
     loads[0].wait()
     loads[1].wait()
     in_part = jnp.dot(
         acts[...].reshape(rows, acts.shape[2]), inb[...], preferred_element_type=F32
     )
-    in_send[...] = in_part.astype(BF16)
+    in_send[...] = in_part
 
     def rows_of(p):
         return pl.ds(pl.multiple_of(p * prow, prow), prow)
@@ -163,20 +171,25 @@
     def sum_in():
         panels(lambda p: a_from(p).wait_recv())
         in_recv[panel] = in_send[rows_of(panel), :]
-        total = in_recv[0].astype(F32)
+        total = in_recv[0]
         for p in range(1, np_):
-            total = total + in_recv[p].astype(F32)
+            total = total + in_recv[p]
         pin[rows_of(panel), :] = total.astype(BF16)
         panels(lambda p: g_copy(p).start())
 
     def weigh():
         loads[2].wait()
         inverse = 1.0 / (eig_ref[...] + DAMPING)
-        for q in range(0, queries, 8):
-            w = qrot[q : q + 8].astype(F32) * inverse[None]
+
+        @pl.loop(0, queries // 8)
+        def _(q8):
+            at = pl.ds(pl.multiple_of(q8 * 8, 8), 8)
+            w = qrot[at].astype(F32) * inverse[None]
             w = w.astype(BF16).astype(F32)
-            weight[:, q : q + 8, :] = jnp.swapaxes(w, 0, 1)
+            weight[:, at, :] = jnp.swapaxes(w, 0, 1)
+
         s_send[...] = jnp.zeros_like(s_send)
+        proj[...] = jnp.zeros_like(proj)
         for copy in grad_loads:
             copy.wait()
 
@@ -189,15 +202,12 @@
             at = pl.ds(s * length, length)
             pinv[at, :] = pin[at, :] * keep
 
-    def add_proj(d, part_rows, at, first):
-        value = lax.dot_general(
-            grads[:, :, at].reshape(rows, at.size), basis[part_rows, at], NT,
+    def add_proj(d, part_rows, j):
+        at = pl.ds(pl.multiple_of(j * cw, cw), cw)
+        proj[d] += lax.dot_general(
+            grads[:, :, at].reshape(rows, cw), basis[j, part_rows], NT,
             preferred_element_type=F32,
         )
-        if first:
-            proj[d] = value
-        else:
-            proj[d] += value
 
     def pair_rows(t):
         return pl.ds(pl.multiple_of(t * pair, pair), pair)
@@ -229,37 +239,51 @@
                 m_recv[p] = m_send[p]
 
     def own_proj():
-        own_load.wait()
         own_copy.wait_recv()
-        for g in range(ngrad):
-            add_proj(0, pair_rows(tok), pl.ds(g * gstep, gstep), g == 0)
+
+        @pl.loop(0, 2 * nc)
+        def _(j):
+            add_proj(0, pair_rows(tok), j)
 
     def own_mix():
         valid_in()
         mix(0, tok)
 
-    tasks = {0: [weigh], min(1, nc - 1): [sum_in], min(2, nc - 1): [own_proj]}
-    tasks.setdefault(min(4, nc - 1), []).append(own_mix)
-    for i in range(nc):
-        for d in range(nt - 1):
-            x_arrive = remote(
-                basis_hbm.at[:, lanes(grp, i)], basis.at[block(from_tok(d), rep), lanes(grp, i)],
-                x_send.at[d, i], x_recv.at[d, i], {"tok": from_tok(d)},
-            )
-            x_arrive.wait_recv()
-            y_copy(d, i, grp).start()
-            cx_copy(d, i, rep).start()
-        for task in tasks.get(i, ()):
-            task()
-        for d in range(nt - 1):
-            y_copy(d, i, 1 - grp).wait_recv()
-            cy_copy(d, i, rep).start()
-        for d in range(nt - 1):
-            t = from_tok(d)
-            cx_copy(d, i, 1 - rep).wait_recv()
-            add_proj(d + 1, pair_rows(t), lanes(grp, i), i == 0)
-            cy_copy(d, i, 1 - rep).wait_recv()
-            add_proj(d + 1, pair_rows(t), lanes(1 - grp, i), False)
+    tasks = {}
+    for turn, task in enumerate((weigh, sum_in, own_proj, own_mix)):
+        tasks.setdefault(min(turn, nc - 1), []).append(task)
+
+    @pl.loop(0, nc + 2)
+    def _(i):
+        @pl.when(i < nc)
+        def _():
+            for d in range(nt - 1):
+                pass_copy(d, i, grp, rep, x_send, x_recv, {"tok": from_tok(d)}).wait_recv()
+                y_copy(d, i, grp).start()
+                cx_copy(d, i, rep).start()
+
+        @pl.when((i > 0) & (i <= nc))
+        def _():
+            for d in range(nt - 1):
+                y_copy(d, i - 1, 1 - grp).wait_recv()
+                cy_copy(d, i - 1, rep).start()
+
+        for turn, todo in tasks.items():
+
+            @pl.when(i == turn)
+            def _():
+                for task in todo:
+                    task()
+
+        @pl.when(i > 1)
+        def _():
+            for d in range(nt - 1):
+                t = from_tok(d)
+                cx_copy(d, i - 2, 1 - rep).wait_recv()
+                add_proj(d + 1, pair_rows(t), grp * nc + i - 2)
+                cy_copy(d, i - 2, 1 - rep).wait_recv()
+                add_proj(d + 1, pair_rows(t), (1 - grp) * nc + i - 2)
+
     for d in range(nt - 1):
         mix(d + 1, from_tok(d))
 
@@ -306,25 +330,15 @@
     each(np_ * nt - 1, lambda index: s_copy(index).start())
     s_recv[me] = s_send[...]
     each(np_ * nt - 1, lambda index: s_from(index).wait_recv())
-    scores = s_recv[0]
+    total = s_recv[0]
     for who in range(1, np_ * nt):
-        scores = scores + s_recv[who]
-    scores = scores[:, 0:queries]
-    score_ref[...] = scores[0:seqs, :]
-    hot = jnp.where(
-        lax.broadcasted_iota(jnp.int32, (NFAIL, queries), 0) == fail_ref[...], 1.0, 0.0
-    )
-    sums_f = lax.dot_general(
-        scores, hot, NT, precision=lax.Precision.HIGHEST, preferred_element_type=F32
-    )
-    counts = lax.dot_general(
-        jnp.ones((8, queries), F32), hot, NT, precision=lax.Precision.HIGHEST,
-        preferred_element_type=F32,
-    )
-    infl_ref[...] = (sums_f / jnp.maximum(counts, 1.0))[0:seqs, :]
+        total = total + s_recv[who]
+    total_ref[...] = total
 
     own_copy.wait_send()
-    for i in range(nc):
+
+    @pl.loop(0, nc)
+    def _(i):
         for d in range(nt - 1):
             x_copy(d, i).wait_send()
             y_copy(d, i, grp).wait_send()
@@ -336,6 +350,23 @@
     each(np_ * nt - 1, lambda index: s_copy(index).wait_send())
 
 
+def finish(total_ref, fail_ref, score_ref, infl_ref):
+    seqs, queries = score_ref.shape
+    scores = total_ref[:, 0:queries]
+    score_ref[...] = scores[0:seqs, :]
+    hot = jnp.where(
+        lax.broadcasted_iota(jnp.int32, (NFAIL, queries), 0) == fail_ref[...], 1.0, 0.0
+    )
+    sums = lax.dot_general(
+        scores, hot, NT, precision=lax.Precision.HIGHEST, preferred_element_type=F32
+    )
+    counts = lax.dot_general(
+        jnp.ones((8, queries), F32), hot, NT, precision=lax.Precision.HIGHEST,
+        preferred_element_type=F32,
+    )
+    infl_ref[...] = (sums / jnp.maximum(counts, 1.0))[0:seqs, :]
+
+
 def per_device(
     np_, nt, grads, acts, out_basis, in_basis, eigvals, query_rot, lengths, token_mask, failure_ids
 ):
@@ -343,7 +374,7 @@
     rows = seqs * length
     queries, kb, ka = query_rot.shape
     cols = out_basis.shape[1]
-    nc = min(8, hidden // 256)
+    nc = min(2, hidden // 256)
     ngrad = min(8, hidden // 256)
     dma = pltpu.SemaphoreType.DMA
     hop = (nt - 1, nc)
@@ -351,12 +382,12 @@
         pltpu.VMEM(grads.shape, BF16),
         pltpu.VMEM(acts.shape, BF16),
         pltpu.VMEM(in_basis.shape, BF16),
-        pltpu.VMEM((cols * nt * 2, hidden), BF16),
+        pltpu.VMEM((2 * nc, cols * nt * 2, hidden // (2 * nc)), BF16),
         pltpu.VMEM(query_rot.shape, BF16),
         pltpu.VMEM((kb, queries, ka), F32),
         pltpu.VMEM((nt, rows, 2 * cols), F32),
-        pltpu.VMEM((rows, ka), BF16),
-        pltpu.VMEM((np_, rows // np_, ka), BF16),
+        pltpu.VMEM((rows, ka), F32),
+        pltpu.VMEM((np_, rows // np_, ka), F32),
         pltpu.VMEM((rows, ka), BF16),
         pltpu.VMEM((rows, ka), BF16),
         pltpu.VMEM((np_, seqs, kb, ka), BF16),
@@ -364,8 +395,9 @@
         pltpu.VMEM((seqs, kb, ka), F32),
         pltpu.VMEM((8, 128), F32),
         pltpu.VMEM((np_ * nt, 8, 128), F32),
-        dma((4,)),
+        dma((3,)),
         dma((ngrad,)),
+        dma((2 * nc,)),
         dma, dma,
         dma(hop), dma(hop), dma(hop), dma(hop),
         dma(hop), dma(hop), dma(hop), dma(hop),
@@ -375,25 +407,29 @@
     ]
     hbm = pl.BlockSpec(memory_space=pl.ANY)
     vmem = pl.BlockSpec(memory_space=pltpu.VMEM)
-    scores, influence = pl.pallas_call(
+    total = pl.pallas_call(
         functools.partial(kernel, (np_, nt, nc, ngrad)),
-        out_shape=(
-            jax.ShapeDtypeStruct((seqs, queries), F32),
-            jax.ShapeDtypeStruct((seqs, NFAIL), F32),
-        ),
-        in_specs=[
-            hbm, hbm, hbm, hbm, vmem, hbm, pl.BlockSpec(memory_space=pltpu.SMEM), vmem, vmem
-        ],
-        out_specs=(vmem, vmem),
+        out_shape=jax.ShapeDtypeStruct((8, 128), F32),
+        in_specs=[hbm, hbm, hbm, hbm, vmem, hbm, pl.BlockSpec(memory_space=pltpu.SMEM), vmem],
+        out_specs=vmem,
         scratch_shapes=scratch,
         compiler_params=pltpu.CompilerParams(
             collective_id=0, has_side_effects=True, vmem_limit_bytes=56 * 1024 * 1024
         ),
         name="influence",
     )(
-        grads, acts, out_basis.T, in_basis, eigvals, query_rot, lengths, token_mask,
-        failure_ids[None, :],
-    )
+        grads, acts, out_basis.T, in_basis, eigvals, query_rot, lengths, token_mask
+    )
+    scores, influence = pl.pallas_call(
+        finish,
+        out_shape=(
+            jax.ShapeDtypeStruct((seqs, queries), F32),
+            jax.ShapeDtypeStruct((seqs, NFAIL), F32),
+        ),
+        in_specs=[vmem, vmem],
+        out_specs=(vmem, vmem),
+        name="finish",
+    )(total, failure_ids[None, :])
     return scores.T, influence.T
 
 

time: 64.8 us -> 43 us (0.66)
  Pallas kernels: 61.5 us -> 42.2 us
  local copies, waits for them, and re-layouts: 2.44 us -> 0 us
    pallas_call x1, Pallas kernels: 61.5 us -> 40.8 us  [per_device(): pl.pallas_call(functools.partial(kernel, (np_, nt, nc, ngrad)), out_shape...]
    unnamed x2 -> x0, local copies, waits for them, and re-layouts: 2.44 us -> none
    pallas_call x0 -> x1, Pallas kernels: none -> 1.39 us  [per_device(): pl.pallas_call(finish, out_shape=(jax.ShapeDtypeStruct((seqs, queries), F...]
where the time goes in v2:
time: 43 us; the launch traced here: 42.8 us
  Pallas kernels  42.2 us (98%)
  between operations  0.64 us (1%)
    pallas_call x1, Pallas kernels, per_device(): pl.pallas_call(functools.partial(kernel, (np_, nt, nc, ngrad)), out_shape...  40.8 us
    pallas_call x1, Pallas kernels, per_device(): pl.pallas_call(finish, out_shape=(jax.ShapeDtypeStruct((seqs, queries), F...  1.39 us

profile of v2, /device:TPU:0, one launch (start us, length us, event | category | flops | bytes accessed | tf_op | source)
XLA Modules:
  0.0 42.8 jit_solution(12862101568414908858)
XLA Ops:
  0.6 40.8 %influence.1.total_ref = f32[8,128]{1,0:T(8,128)} custom-call(bf16[2,256,8192]{2,1,0:T(8,128)(2,1)} %grads_hbm.1, bf16[2,256,2048]{2,1,0:T(8,128)(2,1)} %acts_hbm.1, bf16[64,8192]{1,0:T(8,128)(2,1)} %bitcast.4, bf16[2048,128]{1,0:T(8,128)(2,1)} %inb_hbm.1, f32[64,128]{1,0:T(8,128)} %eig_ref.1, bf16[64,64,128]{2,1,0:T(8,128)(2,1)} %qrot_hbm.1, s32[2]{0:T(128)} %len_ref.1, ...), custom_call_target="tpu_custom_call" | custom-call | tf_op jit(solution)/shard_map/influence/pallas_call | solution.py:410
  41.4 1.4 %finish.1 = (f32[2,64]{1,0:T(2,128)}, f32[2,8]{1,0:T(2,128)}) custom-call(f32[8,128]{1,0:T(8,128)} %influence.1.total_ref, s32[1,64]{1,0:T(1,128)} %bitcast.5), custom_call_target="tpu_custom_call" | custom-call | tf_op jit(solution)/shard_map/finish/pallas_call | solution.py:423

commit v3 on v2

--- a/solution.py
+++ b/solution.py
@@ -205,7 +205,7 @@
     def add_proj(d, part_rows, j):
         at = pl.ds(pl.multiple_of(j * cw, cw), cw)
         proj[d] += lax.dot_general(
-            grads[:, :, at].reshape(rows, cw), basis[j, part_rows], NT,
+            basis[j, part_rows], grads[:, :, at].reshape(rows, cw), NT,
             preferred_element_type=F32,
         )
 
@@ -223,9 +223,7 @@
     def mix(d, t):
         for s in range(seqs):
             at = pl.ds(s * length, length)
-            m = lax.dot_general(
-                proj[d, at, :].astype(BF16), pinv[at, :], TN, preferred_element_type=F32
-            )
+            m = jnp.dot(proj[d, :, at].astype(BF16), pinv[at, :], preferred_element_type=F32)
             m_send[pl.ds(t * npc, npc), s] = m.astype(BF16).reshape(npc, kb, ka)
         for j in range(npc):
             p = t * npc + j
@@ -385,7 +383,7 @@
         pltpu.VMEM((2 * nc, cols * nt * 2, hidden // (2 * nc)), BF16),
         pltpu.VMEM(query_rot.shape, BF16),
         pltpu.VMEM((kb, queries, ka), F32),
-        pltpu.VMEM((nt, rows, 2 * cols), F32),
+        pltpu.VMEM((nt, 2 * cols, rows), F32),
         pltpu.VMEM((rows, ka), F32),
         pltpu.VMEM((np_, rows // np_, ka), F32),
         pltpu.VMEM((rows, ka), BF16),

time: 43 us -> 41.3 us (0.960)
  Pallas kernels: 42.2 us -> 40.4 us
    pallas_call x1, Pallas kernels: 40.8 us -> 39 us  [per_device(): pl.pallas_call(functools.partial(kernel, (np_, nt, nc, ngrad)), out_shape...]
where the time goes in v3:
time: 41.3 us; the launch traced here: 41.1 us
  Pallas kernels  40.4 us (98%)
  between operations  0.64 us (2%)
    pallas_call x1, Pallas kernels, per_device(): pl.pallas_call(functools.partial(kernel, (np_, nt, nc, ngrad)), out_shape...  39 us
    pallas_call x1, Pallas kernels, per_device(): pl.pallas_call(finish, out_shape=(jax.ShapeDtypeStruct((seqs, queries), F...  1.39 us

profile of v3, /device:TPU:0, one launch (start us, length us, event | category | flops | bytes accessed | tf_op | source)
XLA Modules:
  0.0 41.1 jit_solution(16323762365515906104)
XLA Ops:
  0.6 39.0 %influence.1.total_ref = f32[8,128]{1,0:T(8,128)} custom-call(bf16[2,256,8192]{2,1,0:T(8,128)(2,1)} %grads_hbm.1, bf16[2,256,2048]{2,1,0:T(8,128)(2,1)} %acts_hbm.1, bf16[64,8192]{1,0:T(8,128)(2,1)} %bitcast.4, bf16[2048,128]{1,0:T(8,128)(2,1)} %inb_hbm.1, f32[64,128]{1,0:T(8,128)} %eig_ref.1, bf16[64,64,128]{2,1,0:T(8,128)(2,1)} %qrot_hbm.1, s32[2]{0:T(128)} %len_ref.1, ...), custom_call_target="tpu_custom_call" | custom-call | tf_op jit(solution)/shard_map/influence/pallas_call | solution.py:408
  39.7 1.4 %finish.1 = (f32[2,64]{1,0:T(2,128)}, f32[2,8]{1,0:T(2,128)}) custom-call(f32[8,128]{1,0:T(8,128)} %influence.1.total_ref, s32[1,64]{1,0:T(1,128)} %bitcast.5), custom_call_target="tpu_custom_call" | custom-call | tf_op jit(solution)/shard_map/finish/pallas_call | solution.py:421
